TPU v7x, 256 devices: a whole 4x4x8 slice. The times are simulated.
256 devices in a mesh: pts: 32 (over y, x, z_lo), modes: 8 (over z_hi, core).
Axes of the slice: x: 4, y: 4, z: 8 (z_hi: 4, z_lo: 2; z = z_hi * 2 + z_lo), core: 2. Of those that a mesh axis runs over, the one named last changes fastest.
Arguments:
- mode_stress: bfloat16 [6, 4096, 2048], P(None, 'pts', 'modes'), may hold values from -0.125 to 0.125
- histories: bfloat16 [16384, 2048], P(('pts', 'modes')), may hold values from -6 to 6
Outputs:
- peak_mises: float32 [4096], P('pts')
- root_mean: float32 [4096], P('pts')
All inputs are finite; a program needn't handle non-finite values.
Results may differ from a plain program's by a relative error of at most 0.0003.
Values may be sent and summed in bfloat16 or wider, within the bound.
A program may use at most 128 MiB of HBM per device.

v0:
```python
import jax
import jax.numpy as jnp
from jax import lax
from jax.sharding import PartitionSpec as P

STEPS = 16384


def squared_mises(stress):
    sxx, syy, szz = (stress[0], stress[1], stress[2])
    normal = (sxx - syy) ** 2 + (syy - szz) ** 2 + (szz - sxx) ** 2
    shear = stress[3] ** 2 + stress[4] ** 2 + stress[5] ** 2
    return 0.5 * normal + 3.0 * shear


def on_device(mode_stress, histories):
    columns = lax.all_gather(histories, "pts", axis=0, tiled=True)
    stress = jnp.einsum(
        "cpm,tm->cpt",
        lax.all_gather(mode_stress, "modes", axis=2, tiled=True),
        columns,
        preferred_element_type=jnp.float32,
    )
    squared = squared_mises(stress)
    highest = jnp.max(squared, axis=1)
    summed = jnp.sum(squared, axis=1)
    highest = lax.pmax(highest, "modes")
    summed = lax.psum(summed, "modes")
    return (jnp.sqrt(highest), jnp.sqrt(summed / STEPS + 1e-06))


def solution(mesh):
    placed = (P(None, "pts", "modes"), P(("pts", "modes"), None))
    return jax.shard_map(
        on_device, mesh=mesh, in_specs=placed, out_specs=(P("pts"), P("pts")), check_vma=False
    )
```

profile of v0, /device:TPU:1, one launch (start us, length us, event | category | flops | bytes accessed | tf_op | source)
XLA Modules:
  0.0 304.9 jit_solution(11055345018089593311)
XLA Ops:
  7.2 0.0 all-gather.3.cloned.1.call-start
  7.2 0.7 all-gather.3.cloned.1.call-update
  7.9 0.0 all-gather.5.cloned.1.call-start
  7.9 0.7 all-gather.5.cloned.1.call-update
  8.6 54.3 %all-gather.3.cloned.1.call-done = bf16[6,128,2048]{2,1,0:T(8,128)(2,1)} async-done(((bf16[6,128,256]{2,1,0:T(8,128)(2,1)}), bf16[6,128,2048]{2,1,0:T(8,128)(2,1)}) %all-gather.3.cloned.1.call-update) | async-done | bytes 3145744 | tf_op jit(solution)/shard_map/all_gather | solution.py:20
  62.9 192.2 %all-gather.5.cloned.1.call-done = bf16[2048,2048]{1,0:T(8,128)(2,1)} async-done(((bf16[64,2048]{1,0:T(8,128)(2,1)}), bf16[2048,2048]{1,0:T(8,128)(2,1)}) %all-gather.5.cloned.1.call-update) | async-done | bytes 8388624 | tf_op jit(solution)/shard_map/all_gather | solution.py:17
  255.2 10.1 %fusion = f32[6,128,2048]{2,1,0:T(8,128)S(1)} fusion(bf16[6,128,2048]{2,1,0:T(8,128)(2,1)} %all-gather.3.cloned.1.call-done, bf16[2048,2048]{1,0:T(8,128)(2,1)} %all-gather.5.cloned.1.call-done), kind=kOutput, calls=%fused_computation | convolution fusion | flops 6442450944 | bytes 17825792 | tf_op jit(solution)/shard_map/cpm,tm->cpt/dot_general | solution.py:18
  265.3 0.7 fusion.6
  266.0 14.5 %psum.7 = f32[128]{0:T(128)S(1)} all-reduce(f32[128]{0:T(128)S(1)} %get-tuple-element.2), channel_id=1, replica_groups=mesh['pts'=32,'modes'=8] {'modes'}, use_global_device_ids=true, to_apply=%region_3.0 | all-reduce | flops 128 | bytes 1024 | tf_op jit(solution)/shard_map/psum | solution.py:28
  280.4 0.5 add_sqrt_fusion
  280.9 16.6 %pmax.7 = f32[128]{0:T(128)S(1)} all-reduce(f32[128]{0:T(128)S(1)} %get-tuple-element.3), channel_id=1, replica_groups=mesh['pts'=32,'modes'=8] {'modes'}, use_global_device_ids=true, to_apply=%region_1.0 | all-reduce | flops 128 | bytes 1024 | tf_op jit(solution)/shard_map/pmax | solution.py:27
  297.6 0.5 sqrt.6
Async XLA Ops:
  7.2 55.8 %all-gather.3.cloned.1.call-start = ((), (), s32[]{:S(2)}) async-start(), calls=%async_computation | async-start | bytes 3538944 | tf_op jit(solution)/shard_map/all_gather | solution.py:20
  7.9 247.3 %all-gather.5.cloned.1.call-start = ((), (), s32[]{:S(2)}) async-start(), calls=%async_computation.1 | async-start | bytes 8650752 | tf_op jit(solution)/shard_map/all_gather | solution.py:17
Sparse Core Ops, SparseCore 0:
  9.8 53.0 all-gather.2
  64.7 190.4 all-gather.4
where the time goes:
time: 305 us
  waiting for transfers between devices  248 us (81%)
  blocking collectives  31.1 us (10%)
  between operations  14 us (5%)
  matrix products  10.1 us (3%)
    all_gather x1, waiting for transfers between devices, on_device(): columns = lax.all_gather(histories, 'pts', axis=0, tiled=True)  192 us
    all_gather x1, waiting for transfers between devices, on_device(): lax.all_gather(mode_stress, 'modes', axis=2, tiled=True)  54.3 us
    pmax x1, blocking collectives, on_device(): highest = lax.pmax(highest, 'modes')  16.6 us
    psum x1, blocking collectives, on_device(): summed = lax.psum(summed, 'modes')  14.5 us
    dot_general x1, matrix products, on_device(): jnp.einsum('cpm,tm->cpt', lax.all_gather(mode_stress, 'modes', axis=2, ti...  10.1 us
  transfers between devices with their start and end apart: 2, of which 2 were waited for; matrix products, arithmetic and copies ran while one was open for 0% of the time, Pallas kernels for 0%

commit v1 on v0

v1 whole, which is shorter than its diff:
```python
import jax
import jax.numpy as jnp
from jax import lax
from jax.experimental import pallas as pl
from jax.experimental.pallas import tpu as pltpu
from jax.sharding import PartitionSpec as P

STEPS = 16384
MESH = pl.DeviceIdType.MESH
SIDE = 4
DEPTH = 8
PARTS = 6
POINTS = 128
HALF = 128
ROWS = 32
QUARTER = 16
PLACE = (0, 1, 3, 2)


def kernel(stress_ref, hist_ref, out_ref, sbuf, hbuf, acc, part, inbox, load_sem, send_sem, recv_sem):
    pts, modes = lax.axis_index("pts"), lax.axis_index("modes")
    x, y = lax.rem(pts // 2, SIDE), pts // (2 * SIDE)
    z, core = (modes // 2) * 2 + lax.rem(pts, 2), lax.rem(modes, 2)

    def device(dx=0, dy=0, dz=0, dc=0):
        px, py = lax.rem(x + dx + SIDE, SIDE), lax.rem(y + dy + SIDE, SIDE)
        pz = lax.rem(z + dz + DEPTH, DEPTH)
        pc = 1 - core if dc else core
        return ((py * SIDE + px) * 2 + lax.rem(pz, 2), (pz // 2) * 2 + pc)

    def along(axis, d):
        return device(dx=d) if axis == 0 else device(dy=d)

    copies = {}

    def remote(key, src, dst, target):
        i = len(copies)
        copies[key] = pltpu.make_async_remote_copy(
            src_ref=src, dst_ref=dst, send_sem=send_sem.at[i], recv_sem=recv_sem.at[i],
            device_id=target, device_id_type=MESH,
        )

    for sign in (1, -1):
        for step in range(4):
            source, target = (-sign * step) % DEPTH, (-sign * (step + 1)) % DEPTH
            for half in (0, 1):
                if step == 3 and half != (0 if sign == 1 else 1):
                    continue
                remote(("z", target, half), sbuf.at[source, half, 0], sbuf.at[target, half, 0], device(dz=sign))
    for s in range(DEPTH):
        for half in (0, 1):
            remote(("core", s, half), sbuf.at[s, half, 0], sbuf.at[s, half, 1], device(dc=1))

    def rows(h, second, first, cut):
        block = hbuf.at[PLACE[second], h, first]
        return block if cut is None else block.at[pl.ds(cut * QUARTER, QUARTER)]

    for h in (0, 1):
        for sign in (1, -1):
            near, cut = (-sign) % SIDE, 0 if sign == 1 else 1
            remote(("first", h, near, None), rows(h, 0, 0, None), rows(h, 0, near, None), along(h, sign))
            remote(("first", h, 2, cut), rows(h, 0, near, cut), rows(h, 0, 2, cut), along(h, sign))
            for f in range(SIDE):
                remote(("second", h, f, near, None), rows(h, 0, f, None), rows(h, near, f, None), along(1 - h, sign))
                remote(("second", h, f, 2, cut), rows(h, near, f, cut), rows(h, 2, f, cut), along(1 - h, sign))

    others = [(dz, dc) for dz in range(DEPTH) for dc in (0, 1) if (dz, dc) != (0, 0)]
    for i, (dz, dc) in enumerate(others):
        remote(("part", i), part.at[dz % 2], inbox.at[i], device(dz=dz, dc=dc))

    def start(*keys):
        for key in keys:
            copies[key].start()

    def arrived(*keys):
        for key in keys:
            copies[key].wait_recv()

    seen = set()

    def product(place, count, s):
        base = (lax.rem(z + s, DEPTH) // 2) * (4 * HALF)
        own = pl.multiple_of(base + core * (2 * HALF), 2 * HALF)
        sibling = pl.multiple_of(base + (1 - core) * (2 * HALF), 2 * HALF)
        n = count * 2 * SIDE * ROWS
        left = jnp.concatenate(
            [hbuf[place : place + count, :, :, :, pl.ds(at, 2 * HALF)].reshape(n, 2 * HALF) for at in (own, sibling)],
            axis=1,
        )
        right = jnp.concatenate(
            [sbuf[s, half, c].reshape(PARTS * POINTS, HALF) for c in (0, 1) for half in (0, 1)], axis=1
        )
        return lax.dot_general(left, right, (((1,), (1,)), ((), ())), preferred_element_type=jnp.float32)

    def work(places, slots):
        for place in places:
            for s in slots:
                at = pl.ds(place * 2 * SIDE * ROWS, 2 * SIDE * ROWS)
                value = product(place, 1, s)
                if (s % 2, place) in seen:
                    acc[s % 2, at] += value
                else:
                    acc[s % 2, at] = value
                    seen.add((s % 2, place))

    def squared(value):
        s = [value[:, i * POINTS : (i + 1) * POINTS] for i in range(PARTS)]
        xy, yz, zx = s[0] - s[1], s[1] - s[2], s[2] - s[0]
        return 0.5 * (xy * xy + yz * yz + zx * zx) + 3.0 * (s[3] * s[3] + s[4] * s[4] + s[5] * s[5])

    def reduce(which, last=None):
        highest = jnp.zeros((8, POINTS), jnp.float32)
        summed = jnp.zeros((8, POINTS), jnp.float32)
        n = 2 * SIDE * ROWS
        for place in range(4):
            value = acc[which, pl.ds(place * n, n)]
            if last is not None:
                value = value + product(place, 1, last)
            square = squared(value).reshape(n // 8, 8, POINTS)
            highest = jnp.maximum(highest, jnp.max(square, axis=0))
            summed = summed + jnp.sum(square, axis=0)
        part[which, 0] = highest
        part[which, 1] = summed

    barrier = pltpu.get_barrier_semaphore()
    greeted = [device(dz=dz, dc=dc) for dz, dc in others]
    greeted += [along(axis, sign) for axis in (0, 1) for sign in (1, -1)]
    for other in greeted:
        pl.semaphore_signal(barrier, inc=1, device_id=other, device_id_type=MESH)
    loads = [
        pltpu.make_async_copy(stress_ref.at[:, :, pl.ds(half * HALF, HALF)], sbuf.at[0, half, 0], load_sem.at[half])
        for half in (0, 1)
    ] + [
        pltpu.make_async_copy(hist_ref.at[pl.ds(h * ROWS, ROWS)], hbuf.at[0, h, 0], load_sem.at[2 + h])
        for h in (0, 1)
    ]
    for load in loads:
        load.start()
    for load in loads:
        load.wait()
    pl.semaphore_wait(barrier, len(greeted))

    def ring(step):
        return [(("z", 8 - step, 0), ("z", step, 1)), (("z", 8 - step, 1), ("z", step, 0))]

    def forward(step, turn):
        for _, s, half in ring(step)[turn]:
            arrived(("z", s, half))
            onward = s + 1 if s <= 4 else s - 1
            if ("z", onward, half) in copies and (onward != 4 or (half == 0) == (s > 4)):
                start(("z", onward, half))
            start(("core", s, half))

    def have(s):
        arrived(("core", s, 0), ("core", s, 1))

    start(*ring(1)[0])
    start(*[("first", h, near, None) for near in (3, 1) for h in (0, 1)])
    start(*[("second", h, 0, near, None) for near in (3, 1) for h in (0, 1)])
    start(*ring(1)[1], ("core", 0, 0), ("core", 0, 1))

    cut_of = {3: 0, 1: 1}
    for h in (0, 1):
        for near in (3, 1):
            arrived(("first", h, near, None))
            start(("first", h, 2, cut_of[near]))
    for f in (3, 1):
        for h in (0, 1):
            start(*[("second", h, f, near, None) for near in (3, 1)])
    forward(1, 0)
    for h in (0, 1):
        arrived(("first", h, 2, 0), ("first", h, 2, 1))
        start(*[("second", h, 2, near, None) for near in (3, 1)])

    def fold(f):
        for h in (0, 1):
            for near in (3, 1):
                arrived(("second", h, f, near, None))
                start(("second", h, f, 2, cut_of[near]))

    fold(0)
    forward(1, 1)
    have(0)
    work([0], [0])
    have(1)
    have(7)
    fold(3)
    forward(2, 0)
    work([0], [1, 7])
    fold(1)
    fold(2)
    forward(2, 1)
    work([1, 2], [0, 1, 7])
    forward(3, 0)
    have(2)
    have(6)
    work([0, 1, 2], [2, 6])
    for h in (0, 1):
        for f in range(SIDE):
            arrived(("second", h, f, 2, 0), ("second", h, f, 2, 1))
    work([3], [0, 1, 7, 2, 6])
    forward(3, 1)
    have(3)
    have(5)
    work([0, 1, 2, 3], [3, 5])
    reduce(1)
    for half in (0, 1):
        arrived(("z", 4, half))
        start(("core", 4, half))
    have(4)
    reduce(0, 4)

    parts = [("part", i) for i in range(len(others))]
    start(*parts)
    highest, summed = part[0, 0], part[0, 1]
    for i, key in enumerate(parts):
        arrived(key)
        highest = jnp.maximum(highest, inbox[i, 0])
        summed = summed + inbox[i, 1]
    out_ref[0:1] = jnp.max(highest, axis=0, keepdims=True)
    out_ref[1:2] = jnp.sum(summed, axis=0, keepdims=True)
    for copy in copies.values():
        copy.wait_send()


def on_device(mode_stress, histories):
    n_copies = 14 + 16 + 40 + 15
    out = pl.pallas_call(
        kernel,
        out_shape=jax.ShapeDtypeStruct((2, POINTS), jnp.float32),
        in_specs=[pl.BlockSpec(memory_space=pl.ANY)] * 2,
        out_specs=pl.BlockSpec(memory_space=pltpu.VMEM),
        scratch_shapes=[
            pltpu.VMEM((DEPTH, 2, 2, PARTS, POINTS, HALF), jnp.bfloat16),
            pltpu.VMEM((SIDE, 2, SIDE, ROWS, 2048), jnp.bfloat16),
            pltpu.VMEM((2, 2 * SIDE * SIDE * ROWS, PARTS * POINTS), jnp.float32),
            pltpu.VMEM((2, 2, 8, POINTS), jnp.float32),
            pltpu.VMEM((15, 2, 8, POINTS), jnp.float32),
            pltpu.SemaphoreType.DMA((4,)),
            pltpu.SemaphoreType.DMA((n_copies,)),
            pltpu.SemaphoreType.DMA((n_copies,)),
        ],
        compiler_params=pltpu.CompilerParams(
            collective_id=0, has_side_effects=True, vmem_limit_bytes=48 * 2**20
        ),
        cost_estimate=pl.CostEstimate(
            flops=2 * 1024 * 2048 * 2 * PARTS * POINTS, bytes_accessed=2**20, transcendentals=0
        ),
    )(mode_stress, histories)
    return jnp.sqrt(out[0]), jnp.sqrt(out[1] / STEPS + 1e-06)


def solution(mesh):
    placed = (P(None, "pts", "modes"), P(("pts", "modes"), None))
    return jax.shard_map(
        on_device, mesh=mesh, in_specs=placed, out_specs=(P("pts"), P("pts")), check_vma=False
    )
```

time: 305 us -> 54.2 us (0.18)
  waiting for transfers between devices: 248 us -> 0 us
  Pallas kernels: 0 us -> 51 us
  blocking collectives: 31.1 us -> 0 us
  between operations: 14 us -> 0.65 us
  matrix products: 10.1 us -> 0 us
    all_gather x2 -> x0, waiting for transfers between devices: 247 us -> none  [the longest x1 192 us: on_device(): columns = lax.all_gather(histories, 'pts', axis=0, tiled=True)]
    pallas_call x0 -> x1, Pallas kernels: none -> 51 us  [on_device(): pl.pallas_call(kernel, out_shape=jax.ShapeDtypeStruct((2, POINTS), jnp.fl...]
    pmax x1 -> x0, blocking collectives: 16.6 us -> none  [on_device(): highest = lax.pmax(highest, 'modes')]
    psum x1 -> x0, blocking collectives: 14.5 us -> none  [on_device(): summed = lax.psum(summed, 'modes')]
    dot_general x1 -> x0, matrix products: 10.1 us -> none  [on_device(): jnp.einsum('cpm,tm->cpt', lax.all_gather(mode_stress, 'modes', axis=2, ti...]
  transfers between devices with their start and end apart: 2 -> 0, of which waited for: 2 -> 0; matrix products, arithmetic and copies ran while one was open for 0% -> 0% of each run, Pallas kernels for 0% -> 0%
where the time goes in v1:
time: 54.2 us; the launch traced here: 54.1 us
  Pallas kernels  51 us (94%)
  local copies, waits for them, and re-layouts  1.94 us (4%)
  between operations  0.65 us (1%)
    pallas_call x1, Pallas kernels, on_device(): pl.pallas_call(kernel, out_shape=jax.ShapeDtypeStruct((2, POINTS), jnp.fl...  51 us
    unnamed x4, local copies, waits for them, and re-layouts  1.94 us

profile of v1, /device:TPU:1, one launch (start us, length us, event | category | flops | bytes accessed | tf_op | source)
XLA Modules:
  0.0 54.1 jit_solution(12573864024709497546)
XLA Ops:
  0.6 0.0 copy-start
  0.6 1.0 %copy-done = bf16[6,128,256]{2,1,0:T(8,128)(2,1)S(1)} copy-done((bf16[6,128,256]{2,1,0:T(8,128)(2,1)S(1)}, bf16[6,128,256]{2,1,0:T(8,128)(2,1)}, u32[]{:S(2)}) %copy-start) | copy-done | bytes 393240
  1.6 0.0 copy-start.1
  1.6 0.9 %copy-done.1 = bf16[64,2048]{1,0:T(8,128)(2,1)S(1)} copy-done((bf16[64,2048]{1,0:T(8,128)(2,1)S(1)}, bf16[64,2048]{1,0:T(8,128)(2,1)}, u32[]{:S(2)}) %copy-start.1) | copy-done | bytes 262168
  2.6 51.0 %shard_map.41 = f32[2,128]{1,0:T(2,128)S(1)} custom-call(bf16[6,128,256]{2,1,0:T(8,128)(2,1)S(1)} %copy-done, bf16[64,2048]{1,0:T(8,128)(2,1)S(1)} %copy-done.1), custom_call_target="tpu_custom_call" | custom-call | flops 6442450944 | bytes 1048576 | tf_op jit(solution)/shard_map/pallas_call | solution.py:228
  53.6 0.5 sqrt_bitcast_fusion
Async XLA Ops:
  0.6 1.0 %copy-start = (bf16[6,128,256]{2,1,0:T(8,128)(2,1)S(1)}, bf16[6,128,256]{2,1,0:T(8,128)(2,1)}, u32[]{:S(2)}) copy-start(bf16[6,128,256]{2,1,0:T(8,128)(2,1)} %stress_ref.1) | copy-start | bytes 1179652
  1.6 0.9 %copy-start.1 = (bf16[64,2048]{1,0:T(8,128)(2,1)S(1)}, bf16[64,2048]{1,0:T(8,128)(2,1)}, u32[]{:S(2)}) copy-start(bf16[64,2048]{1,0:T(8,128)(2,1)} %hist_ref.1) | copy-start | bytes 786436

commit v2 on v1

v2 whole, which is shorter than its diff:
```python
import jax
import jax.numpy as jnp
from jax import lax
from jax.experimental import pallas as pl
from jax.experimental.pallas import tpu as pltpu
from jax.sharding import PartitionSpec as P

STEPS = 16384
MESH = pl.DeviceIdType.MESH
SIDE = 4
DEPTH = 8
PARTS = 6
POINTS = 128
SHARE = 256
ROWS = 32
QUARTER = 16
GROUP = 2 * SIDE * ROWS
PLACE = (0, 1, 3, 2)


def kernel(stress_ref, hist_ref, out_ref, sbuf, hbuf, acc, part, inbox, load_sem, send_sem, recv_sem):
    pts, modes = lax.axis_index("pts"), lax.axis_index("modes")
    x, y = lax.rem(pts // 2, SIDE), pts // (2 * SIDE)
    z, core = (modes // 2) * 2 + lax.rem(pts, 2), lax.rem(modes, 2)

    def device(dx=0, dy=0, dz=0, dc=0):
        px, py = lax.rem(x + dx + SIDE, SIDE), lax.rem(y + dy + SIDE, SIDE)
        pz = lax.rem(z + dz + DEPTH, DEPTH)
        pc = 1 - core if dc else core
        return ((py * SIDE + px) * 2 + lax.rem(pz, 2), (pz // 2) * 2 + pc)

    def along(axis, d):
        return device(dx=d) if axis == 0 else device(dy=d)

    copies = {}

    def remote(key, src, dst, target):
        i = len(copies)
        copies[key] = pltpu.make_async_remote_copy(
            src_ref=src, dst_ref=dst, send_sem=send_sem.at[i], recv_sem=recv_sem.at[i],
            device_id=target, device_id_type=MESH,
        )

    def piece(s, c, low, n):
        return sbuf.at[s, c, pl.ds(low, n)]

    cuts = {s: ((0, 3), (3, 3)) for s in range(DEPTH)}
    cuts[0] = ((0, 6),)
    cuts[4] = tuple((i, 1) for i in range(PARTS))
    for sign in (1, -1):
        for step in range(4):
            source, target = (-sign * step) % DEPTH, (-sign * (step + 1)) % DEPTH
            for low, n in cuts[target]:
                if step == 3 and (low < 3) != (sign == 1):
                    continue
                remote(("z", target, low), piece(source, 0, low, n), piece(target, 0, low, n), device(dz=sign))
    for s in range(DEPTH):
        for low, n in cuts[s]:
            remote(("core", s, low), piece(s, 0, low, n), piece(s, 1, low, n), device(dc=1))

    def rows(h, second, first, cut):
        block = hbuf.at[PLACE[second], h, first]
        return block if cut is None else block.at[pl.ds(cut * QUARTER, QUARTER)]

    for h in (0, 1):
        for sign in (1, -1):
            near, cut = (-sign) % SIDE, 0 if sign == 1 else 1
            remote(("first", h, near, None), rows(h, 0, 0, None), rows(h, 0, near, None), along(h, sign))
            remote(("first", h, 2, cut), rows(h, 0, near, cut), rows(h, 0, 2, cut), along(h, sign))
            for f in range(SIDE):
                remote(("second", h, f, near, None), rows(h, 0, f, None), rows(h, near, f, None), along(1 - h, sign))
                remote(("second", h, f, 2, cut), rows(h, near, f, cut), rows(h, 2, f, cut), along(1 - h, sign))

    others = [(dz, dc) for dz in (4, 3, 5, 2, 6, 1, 7, 0) for dc in (0, 1) if (dz, dc) != (0, 0)]
    for i, (dz, dc) in enumerate(others):
        remote(("part", i), part.at[dz % 2], inbox.at[i], device(dz=dz, dc=dc))

    def start(*keys):
        for key in keys:
            copies[key].start()

    def arrived(*keys):
        for key in keys:
            copies[key].wait_recv()

    seen = set()

    def product(place, count, s, parts, shares=(0, 1)):
        base = (lax.rem(z + s, DEPTH) // 2) * (2 * SHARE)
        left, right = [], []
        for c in shares:
            first = pl.multiple_of(base + (1 - core if c else core) * SHARE, SHARE)
            left.append(hbuf[place : place + count, :, :, :, pl.ds(first, SHARE)].reshape(count * GROUP, SHARE))
            right.append(jnp.concatenate([sbuf[s, c, i] for i in parts], axis=0))
        left, right = (v[0] if len(v) == 1 else jnp.concatenate(v, axis=1) for v in (left, right))
        return lax.dot_general(left, right, (((1,), (1,)), ((), ())), preferred_element_type=jnp.float32)

    def work(place, count, slots, parts=tuple(range(PARTS)), shares=(0, 1)):
        at = pl.ds(place * GROUP, count * GROUP)
        for s in slots:
            value = product(place, count, s, parts, shares)
            for k, i in enumerate(parts):
                lanes, term = pl.ds(i * POINTS, POINTS), value[:, k * POINTS : (k + 1) * POINTS]
                blocks = {(s % 2, p, i) for p in range(place, place + count)}
                assert blocks <= seen or not blocks & seen
                if blocks <= seen:
                    acc[s % 2, at, lanes] += term
                else:
                    acc[s % 2, at, lanes] = term
                seen.update(blocks)

    def squared(s):
        xy, yz, zx = s[0] - s[1], s[1] - s[2], s[2] - s[0]
        return 0.5 * (xy * xy + yz * yz + zx * zx) + 3.0 * (s[3] * s[3] + s[4] * s[4] + s[5] * s[5])

    def reduce(which, last=()):
        highest = jnp.zeros((8, POINTS), jnp.float32)
        summed = jnp.zeros((8, POINTS), jnp.float32)
        for place in range(4):
            value = [acc[which, pl.ds(place * GROUP, GROUP), pl.ds(i * POINTS, POINTS)] for i in range(PARTS)]
            if last:
                rest = product(place, 1, 4, last, (1,))
                for k, i in enumerate(last):
                    value[i] = value[i] + rest[:, k * POINTS : (k + 1) * POINTS]
            square = squared(value).reshape(GROUP // 8, 8, POINTS)
            highest = jnp.maximum(highest, jnp.max(square, axis=0))
            summed = summed + jnp.sum(square, axis=0)
        part[which, 0:1] = jnp.max(highest, axis=0, keepdims=True)
        part[which, 1:2] = jnp.sum(summed, axis=0, keepdims=True)

    loads = [
        pltpu.make_async_copy(stress_ref.at[pl.ds(low, 3)], piece(0, 0, low, 3), load_sem.at[i])
        for i, low in enumerate((0, 3))
    ] + [
        pltpu.make_async_copy(hist_ref.at[pl.ds(h * ROWS, ROWS)], hbuf.at[0, h, 0], load_sem.at[2 + h])
        for h in (0, 1)
    ]
    for load in loads:
        load.start()
    barrier = pltpu.get_barrier_semaphore()
    greeted = [device(dz=1), device(dz=-1), device(dc=1)]
    greeted += [along(axis, sign) for axis in (0, 1) for sign in (1, -1)]
    for other in greeted:
        pl.semaphore_signal(barrier, inc=1, device_id=other, device_id_type=MESH)
    for load in loads:
        load.wait()
    pl.semaphore_wait(barrier, len(greeted))

    def ring(step):
        return [((8 - step, 0), (step, 3)), ((8 - step, 3), (step, 0))]

    def forward(step, turn):
        for s, low in ring(step)[turn]:
            arrived(("z", s, low))
            if step < 3:
                start(("z", s + 1 if s < 4 else s - 1, low))
            elif turn == 0:
                start(*[("z", 4, low + i) for i in range(3)])
        start(*[("core", s, low) for s, low in ring(step)[turn]])

    def have(s):
        arrived(*[("core", s, low) for low, _ in cuts[s]])

    start(("z", 7, 0), ("z", 1, 3))
    start(*[("first", h, near, None) for near in (3, 1) for h in (0, 1)])
    start(("z", 7, 3), ("z", 1, 0))
    start(*[("second", h, 0, near, None) for near in (3, 1) for h in (0, 1)])
    start(("core", 0, 0))

    cut_of = {3: 0, 1: 1}
    for h in (0, 1):
        for near in (3, 1):
            arrived(("first", h, near, None))
            start(("first", h, 2, cut_of[near]))
    for f in (3, 1):
        for h in (0, 1):
            start(*[("second", h, f, near, None) for near in (3, 1)])
    forward(1, 0)
    for h in (0, 1):
        arrived(("first", h, 2, 0), ("first", h, 2, 1))
        start(*[("second", h, 2, near, None) for near in (3, 1)])

    def fold(f):
        for h in (0, 1):
            for near in (3, 1):
                arrived(("second", h, f, near, None))
                start(("second", h, f, 2, cut_of[near]))

    fold(0)
    forward(1, 1)
    have(0)
    work(0, 1, [0])
    have(1)
    have(7)
    fold(3)
    forward(2, 0)
    work(0, 1, [1, 7])
    fold(1)
    forward(2, 1)
    fold(2)
    work(1, 2, [0, 1, 7])
    have(2)
    have(6)
    work(0, 3, [2, 6])
    forward(3, 0)
    for h in (0, 1):
        for f in range(SIDE):
            arrived(("second", h, f, 2, 0), ("second", h, f, 2, 1))
    work(3, 1, [0, 1, 7, 2, 6])
    arrived(("core", 5, 0), ("core", 3, 3))
    work(0, 4, [5], (0, 1, 2))
    work(0, 4, [3], (3, 4, 5))
    forward(3, 1)
    arrived(("core", 5, 3), ("core", 3, 0))
    work(0, 4, [5], (3, 4, 5))
    work(0, 4, [3], (0, 1, 2))
    for i in range(3):
        for low in (i, 3 + i):
            arrived(("z", 4, low))
            start(("core", 4, low))
        if i:
            arrived(("core", 4, i - 1), ("core", 4, i + 2))
            work(0, 4, [4], (i - 1, i + 2), (1,))
        work(0, 4, [4], (i, 3 + i), (0,))
    reduce(1)
    start(*[("part", i) for i, (dz, _) in enumerate(others) if dz % 2])
    arrived(("core", 4, 2), ("core", 4, 5))
    reduce(0, (2, 5))

    start(*[("part", i) for i, (dz, _) in enumerate(others) if dz % 2 == 0])
    arrived(*[("part", i) for i in range(len(others))])
    out_ref[0:1] = jnp.max(
        jnp.concatenate([part[0, 0:1]] + [inbox[i, 0:1] for i in range(len(others))]), axis=0, keepdims=True
    )
    out_ref[1:2] = jnp.sum(
        jnp.concatenate([part[0, 1:2]] + [inbox[i, 1:2] for i in range(len(others))]), axis=0, keepdims=True
    )
    for copy in copies.values():
        copy.wait_send()


def on_device(mode_stress, histories):
    n_copies = 18 + 19 + 40 + 15
    out = pl.pallas_call(
        kernel,
        out_shape=jax.ShapeDtypeStruct((2, POINTS), jnp.float32),
        in_specs=[pl.BlockSpec(memory_space=pl.ANY)] * 2,
        out_specs=pl.BlockSpec(memory_space=pltpu.VMEM),
        scratch_shapes=[
            pltpu.VMEM((DEPTH, 2, PARTS, POINTS, SHARE), jnp.bfloat16),
            pltpu.VMEM((SIDE, 2, SIDE, ROWS, 2048), jnp.bfloat16),
            pltpu.VMEM((2, 4 * GROUP, PARTS * POINTS), jnp.float32),
            pltpu.VMEM((2, 2, POINTS), jnp.float32),
            pltpu.VMEM((15, 2, POINTS), jnp.float32),
            pltpu.SemaphoreType.DMA((4,)),
            pltpu.SemaphoreType.DMA((n_copies,)),
            pltpu.SemaphoreType.DMA((n_copies,)),
        ],
        compiler_params=pltpu.CompilerParams(
            collective_id=0, has_side_effects=True, vmem_limit_bytes=(53 * 1024 + 816) * 1024
        ),
        cost_estimate=pl.CostEstimate(
            flops=2 * 1024 * 2048 * 2 * PARTS * POINTS, bytes_accessed=2**20, transcendentals=0
        ),
    )(mode_stress, histories)
    return jnp.sqrt(out[0]), jnp.sqrt(out[1] / STEPS + 1e-06)


def solution(mesh):
    placed = (P(None, "pts", "modes"), P(("pts", "modes"), None))
    return jax.shard_map(
        on_device, mesh=mesh, in_specs=placed, out_specs=(P("pts"), P("pts")), check_vma=False
    )
```

time: 54.2 us -> 50.2 us (0.926)
  Pallas kernels: 51 us -> 49 us
  local copies, waits for them, and re-layouts: 1.94 us -> 0 us
    pallas_call x1, Pallas kernels: 51 us -> 49 us  [on_device(): pl.pallas_call(kernel, out_shape=jax.ShapeDtypeStruct((2, POINTS), jnp.fl...]
    unnamed x4 -> x0, local copies, waits for them, and re-layouts: 1.94 us -> none
where the time goes in v2:
time: 50.2 us; the launch traced here: 50.1 us
  Pallas kernels  49 us (98%)
  between operations  0.64 us (1%)
  other arithmetic  0.53 us (1%)
    pallas_call x1, Pallas kernels, on_device(): pl.pallas_call(kernel, out_shape=jax.ShapeDtypeStruct((2, POINTS), jnp.fl...  49 us

profile of v2, /device:TPU:1, one launch (start us, length us, event | category | flops | bytes accessed | tf_op | source)
XLA Modules:
  0.0 50.1 jit_solution(4485049415136592164)
XLA Ops:
  0.6 49.0 %shard_map.41 = f32[2,128]{1,0:T(2,128)S(1)} custom-call(bf16[6,128,256]{2,1,0:T(8,128)(2,1)} %stress_ref.1, bf16[64,2048]{1,0:T(8,128)(2,1)} %hist_ref.1), custom_call_target="tpu_custom_call" | custom-call | flops 6442450944 | bytes 1048576 | tf_op jit(solution)/shard_map/pallas_call | solution.py:244
  49.6 0.5 %sqrt_bitcast_fusion = (f32[128]{0:T(128)}, f32[128]{0:T(128)}) fusion(f32[2,128]{1,0:T(2,128)S(1)} %shard_map.41), kind=kLoop, calls=%fused_computation | loop fusion | flops 256 | bytes 2048 | tf_op jit(solution)/shard_map/sqrt | solution.py:266

commit v3 on v2

--- a/solution.py
+++ b/solution.py
@@ -46,7 +46,8 @@
 
     cuts = {s: ((0, 3), (3, 3)) for s in range(DEPTH)}
     cuts[0] = ((0, 6),)
-    cuts[4] = tuple((i, 1) for i in range(PARTS))
+    cuts[3] = cuts[5] = ((0, 2), (2, 2), (4, 2))
+    cuts[4] = ((0, 2), (2, 1), (3, 1), (4, 2))
     for sign in (1, -1):
         for step in range(4):
             source, target = (-sign * step) % DEPTH, (-sign * (step + 1)) % DEPTH
@@ -128,6 +129,11 @@
         part[which, 0:1] = jnp.max(highest, axis=0, keepdims=True)
         part[which, 1:2] = jnp.sum(summed, axis=0, keepdims=True)
 
+    barrier = pltpu.get_barrier_semaphore()
+    greeted = [device(dz=1), device(dz=-1)] + [along(axis, sign) for axis in (0, 1) for sign in (1, -1)]
+    greeted += [device(dc=1)]
+    for other in greeted:
+        pl.semaphore_signal(barrier, inc=1, device_id=other, device_id_type=MESH)
     loads = [
         pltpu.make_async_copy(stress_ref.at[pl.ds(low, 3)], piece(0, 0, low, 3), load_sem.at[i])
         for i, low in enumerate((0, 3))
@@ -137,31 +143,22 @@
     ]
     for load in loads:
         load.start()
-    barrier = pltpu.get_barrier_semaphore()
-    greeted = [device(dz=1), device(dz=-1), device(dc=1)]
-    greeted += [along(axis, sign) for axis in (0, 1) for sign in (1, -1)]
-    for other in greeted:
-        pl.semaphore_signal(barrier, inc=1, device_id=other, device_id_type=MESH)
-    for load in loads:
-        load.wait()
     pl.semaphore_wait(barrier, len(greeted))
 
-    def ring(step):
-        return [((8 - step, 0), (step, 3)), ((8 - step, 3), (step, 0))]
-
-    def forward(step, turn):
-        for s, low in ring(step)[turn]:
+    def forward(*moves):
+        for s, low, onward in moves:
             arrived(("z", s, low))
-            if step < 3:
-                start(("z", s + 1 if s < 4 else s - 1, low))
-            elif turn == 0:
-                start(*[("z", 4, low + i) for i in range(3)])
-        start(*[("core", s, low) for s, low in ring(step)[turn]])
+            start(*onward)
+        start(*[("core", s, low) for s, low, _ in moves])
 
     def have(s):
         arrived(*[("core", s, low) for low, _ in cuts[s]])
 
+    loads[0].wait()
+    loads[1].wait()
     start(("z", 7, 0), ("z", 1, 3))
+    loads[2].wait()
+    loads[3].wait()
     start(*[("first", h, near, None) for near in (3, 1) for h in (0, 1)])
     start(("z", 7, 3), ("z", 1, 0))
     start(*[("second", h, 0, near, None) for near in (3, 1) for h in (0, 1)])
@@ -175,7 +172,7 @@
     for f in (3, 1):
         for h in (0, 1):
             start(*[("second", h, f, near, None) for near in (3, 1)])
-    forward(1, 0)
+    forward((7, 0, [("z", 6, 0)]), (1, 3, [("z", 2, 3)]))
     for h in (0, 1):
         arrived(("first", h, 2, 0), ("first", h, 2, 1))
         start(*[("second", h, 2, near, None) for near in (3, 1)])
@@ -187,47 +184,53 @@
                 start(("second", h, f, 2, cut_of[near]))
 
     fold(0)
-    forward(1, 1)
+    forward((7, 3, [("z", 6, 3)]), (1, 0, [("z", 2, 0)]))
     have(0)
     work(0, 1, [0])
     have(1)
     have(7)
     fold(3)
-    forward(2, 0)
+    forward((6, 0, [("z", 5, 0)]), (2, 3, [("z", 3, 4)]))
     work(0, 1, [1, 7])
     fold(1)
-    forward(2, 1)
+    forward((6, 3, [("z", 5, 2), ("z", 5, 4)]), (2, 0, [("z", 3, 2), ("z", 3, 0)]))
     fold(2)
     work(1, 2, [0, 1, 7])
     have(2)
     have(6)
     work(0, 3, [2, 6])
-    forward(3, 0)
+    forward((5, 0, [("z", 4, 0)]), (3, 4, [("z", 4, 4)]))
     for h in (0, 1):
         for f in range(SIDE):
             arrived(("second", h, f, 2, 0), ("second", h, f, 2, 1))
     work(3, 1, [0, 1, 7, 2, 6])
-    arrived(("core", 5, 0), ("core", 3, 3))
-    work(0, 4, [5], (0, 1, 2))
-    work(0, 4, [3], (3, 4, 5))
-    forward(3, 1)
-    arrived(("core", 5, 3), ("core", 3, 0))
-    work(0, 4, [5], (3, 4, 5))
-    work(0, 4, [3], (0, 1, 2))
-    for i in range(3):
-        for low in (i, 3 + i):
-            arrived(("z", 4, low))
-            start(("core", 4, low))
-        if i:
-            arrived(("core", 4, i - 1), ("core", 4, i + 2))
-            work(0, 4, [4], (i - 1, i + 2), (1,))
-        work(0, 4, [4], (i, 3 + i), (0,))
+    forward((5, 2, [("z", 4, 2)]), (3, 2, [("z", 4, 3)]))
+    arrived(("core", 5, 0), ("core", 3, 4))
+    work(0, 4, [5], (0, 1))
+    work(0, 4, [3], (4, 5))
+    arrived(("core", 5, 2), ("core", 3, 2))
+    work(0, 4, [5, 3], (2, 3))
+    forward((5, 4, []), (3, 0, []))
+    work(0, 4, [5], (4, 5), (0,))
+    work(0, 4, [3], (0, 1), (0,))
+    arrived(("core", 5, 4), ("core", 3, 0))
+    work(0, 4, [5], (4, 5), (1,))
+    work(0, 4, [3], (0, 1), (1,))
     reduce(1)
     start(*[("part", i) for i, (dz, _) in enumerate(others) if dz % 2])
-    arrived(("core", 4, 2), ("core", 4, 5))
-    reduce(0, (2, 5))
+    forward((4, 0, []), (4, 4, []))
+    work(0, 4, [4], (0, 1, 4, 5), (0,))
+    forward((4, 2, []), (4, 3, []))
+    arrived(("core", 4, 0), ("core", 4, 4))
+    work(0, 4, [4], (0, 1, 4, 5), (1,))
+    work(0, 4, [4], (2, 3), (0,))
+    arrived(("core", 4, 2), ("core", 4, 3))
+    reduce(0, (2, 3))
 
     start(*[("part", i) for i, (dz, _) in enumerate(others) if dz % 2 == 0])
+    for key, copy in copies.items():
+        if key[0] != "part" or others[key[1]][0] % 2:
+            copy.wait_send()
     arrived(*[("part", i) for i in range(len(others))])
     out_ref[0:1] = jnp.max(
         jnp.concatenate([part[0, 0:1]] + [inbox[i, 0:1] for i in range(len(others))]), axis=0, keepdims=True
@@ -235,8 +238,9 @@
     out_ref[1:2] = jnp.sum(
         jnp.concatenate([part[0, 1:2]] + [inbox[i, 1:2] for i in range(len(others))]), axis=0, keepdims=True
     )
-    for copy in copies.values():
-        copy.wait_send()
+    for i, (dz, _) in enumerate(others):
+        if dz % 2 == 0:
+            copies["part", i].wait_send()
 
 
 def on_device(mode_stress, histories):

time: 50.2 us -> 49.2 us (0.980)
  Pallas kernels: 49 us -> 47.9 us
    pallas_call x1, Pallas kernels: 49 us -> 47.9 us  [on_device(): pl.pallas_call(kernel, out_shape=jax.ShapeDtypeStruct((2, POINTS), jnp.fl...]
where the time goes in v3:
time: 49.2 us; the launch traced here: 49.1 us
  Pallas kernels  47.9 us (97%)
  between operations  0.64 us (1%)
  other arithmetic  0.53 us (1%)
    pallas_call x1, Pallas kernels, on_device(): pl.pallas_call(kernel, out_shape=jax.ShapeDtypeStruct((2, POINTS), jnp.fl...  47.9 us

profile of v3, /device:TPU:1, one launch (start us, length us, event | category | flops | bytes accessed | tf_op | source)
XLA Modules:
  0.0 49.1 jit_solution(11668861152475965839)
XLA Ops:
  0.6 47.9 %shard_map.41 = f32[2,128]{1,0:T(2,128)S(1)} custom-call(bf16[6,128,256]{2,1,0:T(8,128)(2,1)} %stress_ref.1, bf16[64,2048]{1,0:T(8,128)(2,1)} %hist_ref.1), custom_call_target="tpu_custom_call" | custom-call | flops 6442450944 | bytes 1048576 | tf_op jit(solution)/shard_map/pallas_call | solution.py:248
  48.6 0.5 %sqrt_bitcast_fusion = (f32[128]{0:T(128)}, f32[128]{0:T(128)}) fusion(f32[2,128]{1,0:T(2,128)S(1)} %shard_map.41), kind=kLoop, calls=%fused_computation | loop fusion | flops 256 | bytes 2048 | tf_op jit(solution)/shard_map/sqrt | solution.py:270

commit v4 on v3

--- a/solution.py
+++ b/solution.py
@@ -84,8 +84,6 @@
         for key in keys:
             copies[key].wait_recv()
 
-    seen = set()
-
     def product(place, count, s, parts, shares=(0, 1)):
         base = (lax.rem(z + s, DEPTH) // 2) * (2 * SHARE)
         left, right = [], []
@@ -102,13 +100,21 @@
             value = product(place, count, s, parts, shares)
             for k, i in enumerate(parts):
                 lanes, term = pl.ds(i * POINTS, POINTS), value[:, k * POINTS : (k + 1) * POINTS]
-                blocks = {(s % 2, p, i) for p in range(place, place + count)}
-                assert blocks <= seen or not blocks & seen
-                if blocks <= seen:
-                    acc[s % 2, at, lanes] += term
-                else:
-                    acc[s % 2, at, lanes] = term
-                seen.update(blocks)
+                acc[s % 2, at, lanes] += term
+
+    def work_all(place, count, slot, step, n):
+        def one(k, carry):
+            s = lax.rem(slot + k * step, DEPTH)
+            acc[lax.rem(s, 2), pl.ds(place * GROUP, count * GROUP)] += product(place, count, s, range(PARTS))
+            return carry
+
+        lax.fori_loop(0, n, one, 0)
+
+    def clear(k, carry):
+        acc[k // 4, pl.ds(pl.multiple_of(lax.rem(k, 4) * GROUP, GROUP), GROUP)] = jnp.zeros(
+            (GROUP, PARTS * POINTS), jnp.float32
+        )
+        return carry
 
     def squared(s):
         xy, yz, zx = s[0] - s[1], s[1] - s[2], s[2] - s[0]
@@ -163,6 +169,7 @@
     start(("z", 7, 3), ("z", 1, 0))
     start(*[("second", h, 0, near, None) for near in (3, 1) for h in (0, 1)])
     start(("core", 0, 0))
+    lax.fori_loop(0, 8, clear, 0)
 
     cut_of = {3: 0, 1: 1}
     for h in (0, 1):
@@ -186,25 +193,25 @@
     fold(0)
     forward((7, 3, [("z", 6, 3)]), (1, 0, [("z", 2, 0)]))
     have(0)
-    work(0, 1, [0])
     have(1)
     have(7)
     fold(3)
     forward((6, 0, [("z", 5, 0)]), (2, 3, [("z", 3, 4)]))
-    work(0, 1, [1, 7])
+    work_all(0, 1, 7, 1, 3)
     fold(1)
     forward((6, 3, [("z", 5, 2), ("z", 5, 4)]), (2, 0, [("z", 3, 2), ("z", 3, 0)]))
     fold(2)
-    work(1, 2, [0, 1, 7])
+    work_all(1, 2, 7, 1, 3)
     have(2)
     have(6)
-    work(0, 3, [2, 6])
+    work_all(0, 3, 2, 4, 2)
     forward((5, 0, [("z", 4, 0)]), (3, 4, [("z", 4, 4)]))
     for h in (0, 1):
         for f in range(SIDE):
             arrived(("second", h, f, 2, 0), ("second", h, f, 2, 1))
-    work(3, 1, [0, 1, 7, 2, 6])
+    work_all(3, 1, 7, 1, 3)
     forward((5, 2, [("z", 4, 2)]), (3, 2, [("z", 4, 3)]))
+    work_all(3, 1, 2, 4, 2)
     arrived(("core", 5, 0), ("core", 3, 4))
     work(0, 4, [5], (0, 1))
     work(0, 4, [3], (4, 5))

time: 49.2 us -> 49.1 us (level)
  no operation moved by 1% of the time
where the time goes in v4:
time: 49.1 us; the launch traced here: 49 us
  Pallas kernels  47.9 us (98%)
  between operations  0.64 us (1%)
  other arithmetic  0.53 us (1%)
    pallas_call x1, Pallas kernels, on_device(): pl.pallas_call(kernel, out_shape=jax.ShapeDtypeStruct((2, POINTS), jnp.fl...  47.9 us

profile of v4, /device:TPU:1, one launch (start us, length us, event | category | flops | bytes accessed | tf_op | source)
XLA Modules:
  0.0 49.0 jit_solution(12919644040059876775)
XLA Ops:
  0.6 47.9 %shard_map.41 = f32[2,128]{1,0:T(2,128)S(1)} custom-call(bf16[6,128,256]{2,1,0:T(8,128)(2,1)} %stress_ref.1, bf16[64,2048]{1,0:T(8,128)(2,1)} %hist_ref.1), custom_call_target="tpu_custom_call" | custom-call | flops 6442450944 | bytes 1048576 | tf_op jit(solution)/shard_map/pallas_call | solution.py:255
  48.5 0.5 %sqrt_bitcast_fusion = (f32[128]{0:T(128)}, f32[128]{0:T(128)}) fusion(f32[2,128]{1,0:T(2,128)S(1)} %shard_map.41), kind=kLoop, calls=%fused_computation | loop fusion | flops 256 | bytes 2048 | tf_op jit(solution)/shard_map/sqrt | solution.py:277

commit v5 on v4

--- a/solution.py
+++ b/solution.py
@@ -154,8 +154,7 @@
     def forward(*moves):
         for s, low, onward in moves:
             arrived(("z", s, low))
-            start(*onward)
-        start(*[("core", s, low) for s, low, _ in moves])
+            start(*onward, ("core", s, low))
 
     def have(s):
         arrived(*[("core", s, low) for low, _ in cuts[s]])
@@ -209,9 +208,8 @@
     for h in (0, 1):
         for f in range(SIDE):
             arrived(("second", h, f, 2, 0), ("second", h, f, 2, 1))
-    work_all(3, 1, 7, 1, 3)
+    work_all(3, 1, 6, 1, 5)
     forward((5, 2, [("z", 4, 2)]), (3, 2, [("z", 4, 3)]))
-    work_all(3, 1, 2, 4, 2)
     arrived(("core", 5, 0), ("core", 3, 4))
     work(0, 4, [5], (0, 1))
     work(0, 4, [3], (4, 5))
@@ -223,9 +221,9 @@
     arrived(("core", 5, 4), ("core", 3, 0))
     work(0, 4, [5], (4, 5), (1,))
     work(0, 4, [3], (0, 1), (1,))
+    forward((4, 0, []), (4, 4, []))
     reduce(1)
     start(*[("part", i) for i, (dz, _) in enumerate(others) if dz % 2])
-    forward((4, 0, []), (4, 4, []))
     work(0, 4, [4], (0, 1, 4, 5), (0,))
     forward((4, 2, []), (4, 3, []))
     arrived(("core", 4, 0), ("core", 4, 4))

time: 49.1 us -> 49.3 us (level)
  no operation moved by 1% of the time
where the time goes in v5:
time: 49.3 us; the launch traced here: 49.2 us
  Pallas kernels  48 us (97%)
  between operations  0.64 us (1%)
  other arithmetic  0.53 us (1%)
    pallas_call x1, Pallas kernels, on_device(): pl.pallas_call(kernel, out_shape=jax.ShapeDtypeStruct((2, POINTS), jnp.fl...  48 us

profile of v5, /device:TPU:1, one launch (start us, length us, event | category | flops | bytes accessed | tf_op | source)
XLA Modules:
  0.0 49.2 jit_solution(5256337711510659318)
XLA Ops:
  0.6 48.0 %shard_map.41 = f32[2,128]{1,0:T(2,128)S(1)} custom-call(bf16[6,128,256]{2,1,0:T(8,128)(2,1)} %stress_ref.1, bf16[64,2048]{1,0:T(8,128)(2,1)} %hist_ref.1), custom_call_target="tpu_custom_call" | custom-call | flops 6442450944 | bytes 1048576 | tf_op jit(solution)/shard_map/pallas_call | solution.py:253
  48.6 0.5 %sqrt_bitcast_fusion = (f32[128]{0:T(128)}, f32[128]{0:T(128)}) fusion(f32[2,128]{1,0:T(2,128)S(1)} %shard_map.41), kind=kLoop, calls=%fused_computation | loop fusion | flops 256 | bytes 2048 | tf_op jit(solution)/shard_map/sqrt | solution.py:275
